TPU v7x, 32 devices: a whole 2x2x4 slice. The times are simulated.
32 devices in a mesh: groups: 2 (over y), chan: 4 (over z), space: 2 (over x), dp: 2 (over core).
Axes of the slice: x: 2, y: 2, z: 4, core: 2. Of those that a mesh axis runs over, the one named last changes fastest.
Arguments:
- inputs: bfloat16 [4, 4, 16, 16, 512], P(('groups', 'dp'), 'space', None, None, 'chan'), parts along dimension 0, may hold values from -6 to 6
- weights: bfloat16 [27, 512, 512], P(None, 'chan'), may hold values from -0.0625 to 0.0625
- bias: float32 [512], P('chan'), may hold values from -3 to 3
- upstream: bfloat16 [4, 4, 16, 16, 512], P(('groups', 'dp'), 'space', None, None, 'chan'), parts along dimension 0, may hold values from -6 to 6
Outputs:
- activated: bfloat16 [4, 4, 16, 16, 512], P(('groups', 'dp'), 'space', None, None, 'chan'), parts along dimension 0
- grad_inputs: bfloat16 [4, 4, 16, 16, 512], P(('groups', 'dp'), 'space', None, None, 'chan'), parts along dimension 0
- grad_weights: float32 [54, 512, 512], P('groups', 'chan', ('space', 'dp')), parts along dimension 0
There are 2 independent parts, one for each index of `groups`. A program takes and returns all parts, laid end to end along the dimension named above; an argument that names none is the same for every part. Nothing has to cross between parts.
All inputs are finite; a program needn't handle non-finite values.
Results may differ from a plain program's by a relative error of at most 0.0049.
Values may be sent and summed in bfloat16 or wider, within the bound.
A program may use at most 64 MiB of HBM per device.

v0:
```python
import math
import jax
import jax.numpy as jnp
from jax import lax
from jax.sharding import PartitionSpec as P

tap_offsets = [(a, b, c) for a in (-1, 0, 1) for b in (-1, 0, 1) for c in (-1, 0, 1)]


def extended(array, sides, width):
    for axis, dim in sides:
        size, length = (lax.axis_size(axis), array.shape[dim])
        up = [(i, (i + 1) % size) for i in range(size - 1)]
        down = [(j, i) for i, j in up]
        last = lax.slice_in_dim(array, length - width, length, axis=dim)
        leading = lax.slice_in_dim(array, 0, width, axis=dim)
        before = lax.ppermute(last, axis, up)
        after = lax.ppermute(leading, axis, down)
        array = jnp.concatenate([before, array, after], axis=dim)
    return array


def spatial_pad(volume):
    return jnp.pad(volume, ((0, 0), (0, 0), (1, 1), (1, 1), (0, 0)))


def tap_slice(volume, a, b, c, width_x, width_y, width_z):
    return volume[:, 1 + a : 1 + a + width_x, 1 + b : 1 + b + width_y, 1 + c : 1 + c + width_z]


def local(inputs, weights, bias, upstream):
    batch_size, width_x, width_y, width_z, group_width = inputs.shape
    voxels = batch_size * width_x * width_y * width_z
    tap_count = weights.shape[0]
    outputs_all = weights.shape[2]
    bordered = spatial_pad(extended(inputs, (("space", 1),), 1))
    stacked = jnp.concatenate(
        [
            tap_slice(bordered, a, b, c, width_x, width_y, width_z).reshape(voxels, group_width)
            for a, b, c in tap_offsets
        ],
        axis=1,
    )
    flat_weights = weights.reshape(tap_count * group_width, outputs_all)
    out_share = outputs_all // lax.axis_size("chan")
    summed = lax.psum_scatter(
        lax.dot_general(
            flat_weights, stacked, (((0,), (1,)), ((), ())), preferred_element_type=jnp.float32
        ),
        "chan",
        scatter_dimension=0,
        tiled=True,
    ).T
    preact = summed + bias[None, :]
    gate_value = jax.nn.sigmoid(preact)
    activated = (
        (preact * gate_value)
        .astype(jnp.bfloat16)
        .reshape(batch_size, width_x, width_y, width_z, out_share)
    )
    grad_flat = (
        upstream.reshape(voxels, out_share).astype(jnp.float32)
        * gate_value
        * (1.0 + preact * (1.0 - gate_value))
    )
    grad_pre = grad_flat.astype(jnp.bfloat16).reshape(
        batch_size, width_x, width_y, width_z, out_share
    )
    grad_full = lax.all_gather(grad_pre, "chan", axis=4, tiled=True)
    framed = extended(grad_full, (("space", 1),), 1)
    interior = framed[:, 1:-1].reshape(voxels, outputs_all)
    framed_all = spatial_pad(framed)
    padded_shape = framed_all.shape
    projected = lax.dot_general(
        framed_all.reshape(-1, outputs_all),
        flat_weights,
        (((1,), (1,)), ((), ())),
        preferred_element_type=jnp.float32,
    )
    projected = projected.reshape(
        padded_shape[0], padded_shape[1], padded_shape[2], padded_shape[3], tap_count, group_width
    )
    grad_in = jnp.zeros((batch_size, width_x, width_y, width_z, group_width), jnp.float32)
    for k, (a, b, c) in enumerate(tap_offsets):
        grad_in = (
            grad_in
            + projected[
                :, 1 - a : 1 - a + width_x, 1 - b : 1 - b + width_y, 1 - c : 1 - c + width_z, k, :
            ]
        )
    grad_inputs = grad_in.astype(jnp.bfloat16)
    weight_partial = lax.dot_general(
        stacked, interior, (((0,), (0,)), ((), ())), preferred_element_type=jnp.float32
    )
    weight_partial = weight_partial.reshape(tap_count, group_width, outputs_all)
    reduced = lax.psum_scatter(weight_partial, ("space", "dp"), scatter_dimension=2, tiled=True)
    total_voxels = voxels * lax.axis_size("space") * lax.axis_size("dp")
    grad_weights = reduced * (1.0 / math.sqrt(total_voxels))
    return (activated, grad_inputs, grad_weights)


def solution(mesh):
    return jax.shard_map(
        local,
        mesh=mesh,
        in_specs=(
            P(("groups", "dp"), "space", None, None, "chan"),
            P(None, "chan", None),
            P("chan"),
            P(("groups", "dp"), "space", None, None, "chan"),
        ),
        out_specs=(
            P(("groups", "dp"), "space", None, None, "chan"),
            P(("groups", "dp"), "space", None, None, "chan"),
            P("groups", "chan", ("space", "dp")),
        ),
        check_vma=False,
    )
```

profile of v0, /device:TPU:0, one launch (start us, length us, event | category | flops | bytes accessed | tf_op | source)
XLA Modules:
  0.0 212.0 jit_solution(125363186464683135)
XLA Ops:
  7.2 1.7 fusion.69
  8.9 5.5 %collective-permute-start = (bf16[1,1,16,16,128]{4,3,2,1,0:T(8,128)(2,1)}, bf16[1,1,16,16,128]{4,3,2,1,0:T(8,128)(2,1)}, u32[]{:S(2)}, u32[]{:S(2)}) collective-permute-start(bf16[1,1,16,16,128]{4,3,2,1,0:T(8,128)(2,1)} %get-tuple-element.33), channel_id=1, source_target_pairs={{0,2},{1,3},{4,6},{5,7},{8,10},{9,11},{12,14},{13,15},{16,18},{17,... | collective-permute-start | bytes 196616 | tf_op jit(solution)/shard_map/ppermute | solution.py:17
  14.4 1.3 collective-permute-start.1
  15.6 1.7 copy.20
  17.3 3.5 %collective-permute-done.1 = bf16[1,1,16,16,128]{4,3,2,1,0:T(8,128)(2,1)} collective-permute-done((bf16[1,1,16,16,128]{4,3,2,1,0:T(8,128)(2,1)}, bf16[1,1,16,16,128]{4,3,2,1,0:T(8,128)(2,1)}, u32[]{:S(2)}, u32[]{:S(2)}) %collective-permute-start.1) | collective-permute-done | bytes 65568 | tf_op jit(solution)/shard_map/ppermute | solution.py:18
  20.8 1.1 select_maximum_fusion.3
  22.8 1.5 fusion.67
  24.3 1.6 pad_maximum_fusion
  26.0 1.7 copy.29
  27.6 1.7 copy.11
  29.3 1.7 copy.12
  30.9 1.7 copy.10
  32.6 1.7 copy.9
  34.3 1.7 copy.8
  35.9 1.7 copy.7
  37.6 1.7 copy.33
  39.2 1.7 copy.32
  40.9 1.7 copy.31
  42.6 1.7 copy.30
  44.2 1.7 copy.28
  45.9 1.7 copy.27
  47.6 1.7 copy.26
  49.2 1.7 copy.25
  50.9 1.7 copy.24
  52.5 1.7 copy.23
  54.2 1.7 copy.22
  55.9 1.7 copy.21
  57.5 1.7 copy.19
  59.2 1.7 copy.18
  60.9 1.7 copy.17
  62.5 1.7 copy.16
  64.2 1.7 copy.15
  65.8 1.7 copy.14
  67.5 1.7 copy.13
  82.6 1.9 copy-done.2
  84.5 3.0 %convolution_bitcast_fusion.1 = f32[512,512]{0,1:T(8,128)} fusion(bf16[512,3456]{0,1:T(8,128)(2,1)S(1)} %constant_dynamic-update-slice_fusion, bf16[3456,512]{1,0:T(8,128)(2,1)S(1)} %bitcast.262), kind=kOutput, calls=%fused_computation.21 | convolution fusion | flops 1811939328 | bytes 8126464 | tf_op jit(solution)/shard_map/dot_general | solution.py:47
  87.6 27.6 %reduce-scatter.3.cloned.1.call-done = f32[128,512]{0,1:T(8,128)} async-done(((f32[512,512]{0,1:T(8,128)}), f32[128,512]{0,1:T(8,128)}) %reduce-scatter.3.cloned.1.call-update) | async-done | bytes 262160 | tf_op jit(solution)/shard_map/reduce_scatter | solution.py:46
  115.2 1.8 fusion.56
  117.0 15.3 %all_gather.3 = bf16[1,2,16,16,512]{4,3,2,1,0:T(8,128)(2,1)S(1)} all-gather(bf16[1,2,16,16,128]{4,3,2,1,0:T(8,128)(2,1)S(1)} %bitcast.290), channel_id=1, replica_groups=mesh['groups'=2,'chan'=4,'space'=2,'dp'=2] {'chan'}, dimensions={4}, use_global_device_ids=true | all-gather | bytes 655360 | tf_op jit(solution)/shard_map/all_gather | solution.py:69
  133.1 6.9 %fusion.70 = f32[27,128,512]{2,1,0:T(8,128)} fusion(bf16[27,128,512]{2,1,0:T(8,128)(2,1)} %bitcast.264, bf16[512,512,1]{1,0,2:T(8,128)(2,1)S(1)} %bitcast.263), kind=kOutput, calls=%fused_computation.139 | convolution fusion | flops 1811939328 | bytes 11141120 | tf_op jit(solution)/shard_map/dot_general | solution.py:92
  141.1 3.3 %collective-permute-start.2 = (bf16[1,1,16,16,512]{4,3,2,1,0:T(8,128)(2,1)S(1)}, bf16[1,1,16,16,512]{4,3,2,1,0:T(8,128)(2,1)S(1)}, u32[]{:S(2)}, u32[]{:S(2)}) collective-permute-start(bf16[1,1,16,16,512]{4,3,2,1,0:T(8,128)(2,1)S(1)} %get-tuple-element.3), channel_id=1, source_target_pairs={{0,2},{1,3},{4,6},{5,7},{8,10},{9,11},{12,14},{13,15},{16,18},{17,... | collective-permute-start | bytes 786440 | tf_op jit(solution)/shard_map/ppermute | solution.py:17
  144.4 1.3 collective-permute-start.3
  145.7 2.6 %collective-permute-done.2 = bf16[1,1,16,16,512]{4,3,2,1,0:T(8,128)(2,1)S(1)} collective-permute-done((bf16[1,1,16,16,512]{4,3,2,1,0:T(8,128)(2,1)S(1)}, bf16[1,1,16,16,512]{4,3,2,1,0:T(8,128)(2,1)S(1)}, u32[]{:S(2)}, u32[]{:S(2)}) %collective-permute-start.2) | collective-permute-done | bytes 262176 | tf_op jit(solution)/shard_map/ppermute | solution.py:17
  148.2 4.4 %collective-permute-done.3 = bf16[1,1,16,16,512]{4,3,2,1,0:T(8,128)(2,1)S(1)} collective-permute-done((bf16[1,1,16,16,512]{4,3,2,1,0:T(8,128)(2,1)S(1)}, bf16[1,1,16,16,512]{4,3,2,1,0:T(8,128)(2,1)S(1)}, u32[]{:S(2)}, u32[]{:S(2)}) %collective-permute-start.3) | collective-permute-done | bytes 262176 | tf_op jit(solution)/shard_map/ppermute | solution.py:18
  152.6 8.2 %convolution_bitcast_fusion = f32[1,4,18,18,27,128]{5,3,4,2,1,0:T(8,128)S(1)} fusion(bf16[27,128,512]{2,1,0:T(8,128)(2,1)S(1)} %copy-done, bf16[1,1,16,16,512]{4,3,2,1,0:T(8,128)(2,1)S(1)} %collective-permute-done.3, bf16[1,2,16,16,512]{4,3,2,1,0:T(8,128)(2,1)} %copy-done.1, bf16[1,1,16,16,512]{4,3,2,1,0:T(8,128)(2,1)S(1)} %collective-permute-done.2), kind=kOutput, calls=%fused_computation | convolution fusion | flops 4599078912 | bytes 22503424 | tf_op jit(solution)/shard_map/dot_general | solution.py:74
  160.8 1.2 fusion.28
  162.0 40.2 %reduce-scatter.5.cloned.1.call-done = f32[27,128,128]{2,1,0:T(8,128)} async-done(((f32[27,128,512]{2,1,0:T(8,128)}), f32[27,128,128]{2,1,0:T(8,128)}) %reduce-scatter.5.cloned.1.call-update) | async-done | bytes 1769488 | tf_op jit(solution)/shard_map/reduce_scatter | solution.py:96
  202.2 2.9 %broadcast_multiply_fusion = f32[27,128,128]{2,1,0:T(8,128)} fusion(f32[27,128,128]{2,1,0:T(8,128)} %reduce-scatter.5.cloned.1.call-done), kind=kLoop, calls=%fused_computation.27 | loop fusion | flops 442368 | bytes 3538944 | tf_op jit(solution)/shard_map/mul | solution.py:98
  (69 shorter events, 16.0 us)
Async XLA Ops:
  7.2 75.5 %copy-start = (bf16[27,128,512]{2,1,0:T(8,128)(2,1)S(1)}, bf16[27,128,512]{2,1,0:T(8,128)(2,1)}, u32[]{:S(2)}) copy-start(bf16[27,128,512]{2,1,0:T(8,128)(2,1)} %param.5) | copy-start | bytes 10616836
  7.2 108.0 %reduce-scatter.3.cloned.1.call-start = ((), (), s32[]{:S(2)}) async-start(), calls=%async_computation.2 | async-start | bytes 1310720 | tf_op jit(solution)/shard_map/reduce_scatter | solution.py:46
  8.9 8.4 %collective-permute-start = (bf16[1,1,16,16,128]{4,3,2,1,0:T(8,128)(2,1)}, bf16[1,1,16,16,128]{4,3,2,1,0:T(8,128)(2,1)}, u32[]{:S(2)}, u32[]{:S(2)}) collective-permute-start(bf16[1,1,16,16,128]{4,3,2,1,0:T(8,128)(2,1)} %get-tuple-element.33), channel_id=1, source_target_pairs={{0,2},{1,3},{4,6},{5,7},{8,10},{9,11},{12,14},{13,15},{16,18},{17,... | collective-permute-start | bytes 196616 | tf_op jit(solution)/shard_map/ppermute | solution.py:17
  14.4 6.5 %collective-permute-start.1 = (bf16[1,1,16,16,128]{4,3,2,1,0:T(8,128)(2,1)}, bf16[1,1,16,16,128]{4,3,2,1,0:T(8,128)(2,1)}, u32[]{:S(2)}, u32[]{:S(2)}) collective-permute-start(bf16[1,1,16,16,128]{4,3,2,1,0:T(8,128)(2,1)} %get-tuple-element.34), channel_id=1, source_target_pairs={{2,0},{3,1},{6,4},{7,5},{10,8},{11,9},{14,12},{15,13},{18,16},{19,... | collective-permute-start | bytes 196616 | tf_op jit(solution)/shard_map/ppermute | solution.py:18
  17.3 7.0 %copy-start.3 = (bf16[1,2,16,16,128]{4,3,2,1,0:T(8,128)(2,1)S(1)}, bf16[1,2,16,16,128]{4,3,2,1,0:T(8,128)(2,1)}, u32[]{:S(2)}) copy-start(bf16[1,2,16,16,128]{4,3,2,1,0:T(8,128)(2,1)} %param.4) | copy-start | bytes 393220
  69.2 13.1 %copy-start.16 = (bf16[512,128]{0,1:T(8,128)(2,1)S(1)}, bf16[512,128]{0,1:T(8,128)(2,1)}, u32[]{:S(2)}) copy-start(bf16[512,128]{0,1:T(8,128)(2,1)} %copy.21) | copy-start | bytes 393220
  69.2 13.1 %copy-start.15 = (bf16[512,128]{0,1:T(8,128)(2,1)S(1)}, bf16[512,128]{0,1:T(8,128)(2,1)}, u32[]{:S(2)}) copy-start(bf16[512,128]{0,1:T(8,128)(2,1)} %copy.22) | copy-start | bytes 393220
  69.2 13.2 %copy-start.14 = (bf16[512,128]{0,1:T(8,128)(2,1)S(1)}, bf16[512,128]{0,1:T(8,128)(2,1)}, u32[]{:S(2)}) copy-start(bf16[512,128]{0,1:T(8,128)(2,1)} %copy.23) | copy-start | bytes 393220
  69.2 13.2 %copy-start.13 = (bf16[512,128]{0,1:T(8,128)(2,1)S(1)}, bf16[512,128]{0,1:T(8,128)(2,1)}, u32[]{:S(2)}) copy-start(bf16[512,128]{0,1:T(8,128)(2,1)} %copy.24) | copy-start | bytes 393220
  69.2 13.2 %copy-start.12 = (bf16[512,128]{0,1:T(8,128)(2,1)S(1)}, bf16[512,128]{0,1:T(8,128)(2,1)}, u32[]{:S(2)}) copy-start(bf16[512,128]{0,1:T(8,128)(2,1)} %copy.25) | copy-start | bytes 393220
  69.2 13.2 %copy-start.11 = (bf16[512,128]{0,1:T(8,128)(2,1)S(1)}, bf16[512,128]{0,1:T(8,128)(2,1)}, u32[]{:S(2)}) copy-start(bf16[512,128]{0,1:T(8,128)(2,1)} %copy.26) | copy-start | bytes 393220
  69.2 13.2 %copy-start.10 = (bf16[512,128]{0,1:T(8,128)(2,1)S(1)}, bf16[512,128]{0,1:T(8,128)(2,1)}, u32[]{:S(2)}) copy-start(bf16[512,128]{0,1:T(8,128)(2,1)} %copy.27) | copy-start | bytes 393220
  69.2 13.3 %copy-start.9 = (bf16[512,128]{0,1:T(8,128)(2,1)S(1)}, bf16[512,128]{0,1:T(8,128)(2,1)}, u32[]{:S(2)}) copy-start(bf16[512,128]{0,1:T(8,128)(2,1)} %copy.28) | copy-start | bytes 393220
  69.2 13.3 %copy-start.4 = (bf16[512,128]{0,1:T(8,128)(2,1)S(1)}, bf16[512,128]{0,1:T(8,128)(2,1)}, u32[]{:S(2)}) copy-start(bf16[512,128]{0,1:T(8,128)(2,1)} %copy.29) | copy-start | bytes 393220
  69.2 13.3 %copy-start.8 = (bf16[512,128]{0,1:T(8,128)(2,1)S(1)}, bf16[512,128]{0,1:T(8,128)(2,1)}, u32[]{:S(2)}) copy-start(bf16[512,128]{0,1:T(8,128)(2,1)} %copy.30) | copy-start | bytes 393220
  69.2 13.3 %copy-start.7 = (bf16[512,128]{0,1:T(8,128)(2,1)S(1)}, bf16[512,128]{0,1:T(8,128)(2,1)}, u32[]{:S(2)}) copy-start(bf16[512,128]{0,1:T(8,128)(2,1)} %copy.31) | copy-start | bytes 393220
  69.2 13.3 %copy-start.6 = (bf16[512,128]{0,1:T(8,128)(2,1)S(1)}, bf16[512,128]{0,1:T(8,128)(2,1)}, u32[]{:S(2)}) copy-start(bf16[512,128]{0,1:T(8,128)(2,1)} %copy.32) | copy-start | bytes 393220
  69.2 13.4 %copy-start.5 = (bf16[512,128]{0,1:T(8,128)(2,1)S(1)}, bf16[512,128]{0,1:T(8,128)(2,1)}, u32[]{:S(2)}) copy-start(bf16[512,128]{0,1:T(8,128)(2,1)} %copy.33) | copy-start | bytes 393220
  82.6 1.9 copy-start.2
  84.5 30.7 %copy-start.17 = (f32[128]{0:T(128)S(1)}, f32[128]{0:T(128)}, u32[]{:S(2)}) copy-start(f32[128]{0:T(128)} %param.6) | copy-start | bytes 1540
  87.6 114.6 %reduce-scatter.5.cloned.1.call-start = ((), (), s32[]{:S(2)}) async-start(), calls=%async_computation.3 | async-start | bytes 8847360 | tf_op jit(solution)/shard_map/reduce_scatter | solution.py:96
  132.3 0.8 copy-start.1
  141.1 7.1 %collective-permute-start.2 = (bf16[1,1,16,16,512]{4,3,2,1,0:T(8,128)(2,1)S(1)}, bf16[1,1,16,16,512]{4,3,2,1,0:T(8,128)(2,1)S(1)}, u32[]{:S(2)}, u32[]{:S(2)}) collective-permute-start(bf16[1,1,16,16,512]{4,3,2,1,0:T(8,128)(2,1)S(1)} %get-tuple-element.3), channel_id=1, source_target_pairs={{0,2},{1,3},{4,6},{5,7},{8,10},{9,11},{12,14},{13,15},{16,18},{17,... | collective-permute-start | bytes 786440 | tf_op jit(solution)/shard_map/ppermute | solution.py:17
  144.4 8.3 %collective-permute-start.3 = (bf16[1,1,16,16,512]{4,3,2,1,0:T(8,128)(2,1)S(1)}, bf16[1,1,16,16,512]{4,3,2,1,0:T(8,128)(2,1)S(1)}, u32[]{:S(2)}, u32[]{:S(2)}) collective-permute-start(bf16[1,1,16,16,512]{4,3,2,1,0:T(8,128)(2,1)S(1)} %get-tuple-element.4), channel_id=1, source_target_pairs={{2,0},{3,1},{6,4},{7,5},{10,8},{11,9},{14,12},{15,13},{18,16},{19,... | collective-permute-start | bytes 786440 | tf_op jit(solution)/shard_map/ppermute | solution.py:18
Sparse Core Ops, SparseCore 0:
  87.7 27.4 reduce-scatter.2
  140.1 62.0 reduce-scatter.4
where the time goes:
time: 213 us; the launch traced here: 212 us
  waiting for transfers between devices  78.3 us (37%)
  local copies, waits for them, and re-layouts  65.8 us (31%)
  matrix products  18.1 us (8%)
  blocking collectives  15.3 us (7%)
  between operations  14.5 us (7%)
  starting transfers between devices  11.4 us (5%)
  other arithmetic  8.62 us (4%)
    reshape x27, local copies, waits for them, and re-layouts, local(): tap_slice(bordered, a, b, c, width_x, width_y, width_z)  44.9 us
    reduce_scatter x1, waiting for transfers between devices, local(): lax.psum_scatter(weight_partial, ('space', 'dp'), scatter_dimension=2, ti...  40.2 us
    reduce_scatter x1, waiting for transfers between devices, local(): lax.psum_scatter(lax.dot_general(flat_weights, stacked, (((0,), (1,)), ((...  27.6 us
    unnamed x62, local copies, waits for them, and re-layouts  15.8 us
    all_gather x1, blocking collectives, local(): grad_full = lax.all_gather(grad_pre, 'chan', axis=4, tiled=True)  15.3 us
    ppermute x2, starting transfers between devices, extended(): before = lax.ppermute(last, axis, up)  8.73 us
    dot_general x1, matrix products, local(): lax.dot_general(framed_all.reshape(-1, outputs_all), flat_weights, (((1,)...  8.15 us
    ppermute x2, waiting for transfers between devices, extended(): after = lax.ppermute(leading, axis, down)  7.9 us
  transfers between devices with their start and end apart: 6, of which 5 were waited for; matrix products, arithmetic and copies ran while one was open for 6% of the time, Pallas kernels for 0%

commit v1 on v0

--- a/solution.py
+++ b/solution.py
@@ -66,7 +66,15 @@
     grad_pre = grad_flat.astype(jnp.bfloat16).reshape(
         batch_size, width_x, width_y, width_z, out_share
     )
-    grad_full = lax.all_gather(grad_pre, "chan", axis=4, tiled=True)
+    ways, here = (lax.axis_size("chan"), lax.axis_index("chan"))
+    grown, reach = (grad_pre, 1)
+    while reach < ways:
+        theirs = lax.ppermute(grown, "chan", [(d, d ^ reach) for d in range(ways)])
+        mine_first = jnp.concatenate([grown, theirs], axis=4)
+        theirs_first = jnp.concatenate([theirs, grown], axis=4)
+        grown = jnp.where(here & reach == 0, mine_first, theirs_first)
+        reach = 2 * reach
+    grad_full = grown
     framed = extended(grad_full, (("space", 1),), 1)
     interior = framed[:, 1:-1].reshape(voxels, outputs_all)
     framed_all = spatial_pad(framed)

time: 213 us -> 218 us (1.023)
  waiting for transfers between devices: 78.3 us -> 94.7 us
  blocking collectives: 15.3 us -> 0 us
  other arithmetic: 8.62 us -> 14 us
    ppermute x0 -> x2, waiting for transfers between devices: none -> 16.8 us  [local(): theirs = lax.ppermute(grown, 'chan', [(d, d ^ reach) for d in range(ways)])]
    all_gather x1 -> x0, blocking collectives: 15.3 us -> none  [local(): grad_full = lax.all_gather(grad_pre, 'chan', axis=4, tiled=True)]
    select_n x0 -> x3, other arithmetic: none -> 4.2 us  [local(): grown = jnp.where(here & reach == 0, mine_first, theirs_first)]
    unnamed x62 -> x60, local copies, waits for them, and re-layouts: 15.8 us -> 15 us
  transfers between devices with their start and end apart: 6 -> 8, of which waited for: 5 -> 7; matrix products, arithmetic and copies ran while one was open for 6% -> 6% of each run, Pallas kernels for 0% -> 0%
where the time goes in v1:
time: 218 us; the launch traced here: 217 us
  waiting for transfers between devices  94.7 us (43%)
  local copies, waits for them, and re-layouts  63.9 us (29%)
  matrix products  16.7 us (8%)
  between operations  14.5 us (7%)
  other arithmetic  14 us (6%)
  starting transfers between devices  12.9 us (6%)
    reshape x27, local copies, waits for them, and re-layouts, local(): tap_slice(bordered, a, b, c, width_x, width_y, width_z)  44.7 us
    reduce_scatter x1, waiting for transfers between devices, local(): lax.psum_scatter(weight_partial, ('space', 'dp'), scatter_dimension=2, ti...  38.5 us
    reduce_scatter x1, waiting for transfers between devices, local(): lax.psum_scatter(lax.dot_general(flat_weights, stacked, (((0,), (1,)), ((...  27.6 us
    ppermute x2, waiting for transfers between devices, local(): theirs = lax.ppermute(grown, 'chan', [(d, d ^ reach) for d in range(ways)])  16.8 us
    unnamed x60, local copies, waits for them, and re-layouts  15 us
    ppermute x2, starting transfers between devices, extended(): before = lax.ppermute(last, axis, up)  8.84 us
    ppermute x2, waiting for transfers between devices, extended(): after = lax.ppermute(leading, axis, down)  7.64 us
    dot_general x1, matrix products, local(): lax.dot_general(stacked, interior, (((0,), (0,)), ((), ())), preferred_el...  6.97 us
  transfers between devices with their start and end apart: 8, of which 7 were waited for; matrix products, arithmetic and copies ran while one was open for 6% of the time, Pallas kernels for 0%

profile of v1, /device:TPU:0, one launch (start us, length us, event | category | flops | bytes accessed | tf_op | source)
XLA Modules:
  0.0 216.8 jit_solution(15230322517483690376)
XLA Ops:
  7.2 1.7 fusion.80
  8.9 5.5 %collective-permute-start = (bf16[1,1,16,16,128]{4,3,2,1,0:T(8,128)(2,1)}, bf16[1,1,16,16,128]{4,3,2,1,0:T(8,128)(2,1)}, u32[]{:S(2)}, u32[]{:S(2)}) collective-permute-start(bf16[1,1,16,16,128]{4,3,2,1,0:T(8,128)(2,1)} %get-tuple-element.33), channel_id=1, source_target_pairs={{0,2},{1,3},{4,6},{5,7},{8,10},{9,11},{12,14},{13,15},{16,18},{17,... | collective-permute-start | bytes 196616 | tf_op jit(solution)/shard_map/ppermute | solution.py:17
  14.4 1.3 collective-permute-start.1
  15.7 1.7 copy.20
  17.3 3.5 %collective-permute-done.1 = bf16[1,1,16,16,128]{4,3,2,1,0:T(8,128)(2,1)} collective-permute-done((bf16[1,1,16,16,128]{4,3,2,1,0:T(8,128)(2,1)}, bf16[1,1,16,16,128]{4,3,2,1,0:T(8,128)(2,1)}, u32[]{:S(2)}, u32[]{:S(2)}) %collective-permute-start.1) | collective-permute-done | bytes 65568 | tf_op jit(solution)/shard_map/ppermute | solution.py:18
  22.8 1.5 fusion.78
  24.4 1.6 pad_maximum_fusion
  26.0 1.7 copy.29
  27.6 1.7 copy.11
  29.3 1.7 copy.12
  30.9 1.7 copy.10
  32.6 1.6 copy.9
  34.2 1.7 copy.8
  35.9 1.7 copy.7
  37.6 1.7 copy.33
  39.2 1.7 copy.32
  40.9 1.7 copy.31
  42.6 1.7 copy.30
  44.2 1.7 copy.28
  45.9 1.7 copy.27
  47.5 1.7 copy.26
  49.2 1.7 copy.25
  50.8 1.6 copy.24
  52.5 1.7 copy.23
  54.2 1.7 copy.22
  55.8 1.6 copy.21
  57.5 1.6 copy.19
  59.1 1.7 copy.18
  60.8 1.7 copy.17
  62.4 1.7 copy.16
  64.1 1.7 copy.15
  65.7 1.6 copy.14
  67.4 1.7 copy.13
  82.5 1.9 copy-done.1
  84.4 3.0 %convolution_bitcast_fusion.1 = f32[512,512]{0,1:T(8,128)} fusion(bf16[512,3456]{0,1:T(8,128)(2,1)S(1)} %constant_dynamic-update-slice_fusion, bf16[3456,512]{1,0:T(8,128)(2,1)S(1)} %bitcast.267), kind=kOutput, calls=%fused_computation.21 | convolution fusion | flops 1811939328 | bytes 8126464 | tf_op jit(solution)/shard_map/dot_general | solution.py:47
  87.5 27.6 %reduce-scatter.3.cloned.1.call-done = f32[128,512]{0,1:T(8,128)} async-done(((f32[512,512]{0,1:T(8,128)}), f32[128,512]{0,1:T(8,128)}) %reduce-scatter.3.cloned.1.call-update) | async-done | bytes 262160 | tf_op jit(solution)/shard_map/reduce_scatter | solution.py:46
  115.1 1.8 fusion.66
  116.9 5.4 %collective-permute-done.2 = bf16[1,2,16,16,128]{4,3,2,1,0:T(8,128)(2,1)} collective-permute-done((bf16[1,2,16,16,128]{4,3,2,1,0:T(8,128)(2,1)}, bf16[1,2,16,16,128]{4,3,2,1,0:T(8,128)(2,1)}, u32[]{:S(2)}, u32[]{:S(2)}) %collective-permute-start.2) | collective-permute-done | bytes 131104 | tf_op jit(solution)/shard_map/ppermute | solution.py:72
  122.3 1.9 maximum_select_fusion.3
  126.6 11.4 %collective-permute-done.3 = bf16[1,2,16,16,256]{4,3,2,1,0:T(8,128)(2,1)} collective-permute-done((bf16[1,2,16,16,256]{4,3,2,1,0:T(8,128)(2,1)}, bf16[1,2,16,16,256]{4,3,2,1,0:T(8,128)(2,1)}, u32[]{:S(2)}, u32[]{:S(2)}) %collective-permute-start.3) | collective-permute-done | bytes 262176 | tf_op jit(solution)/shard_map/ppermute | solution.py:72
  138.0 7.0 %fusion.25 = f32[27,128,512]{2,1,0:T(8,128)} fusion(bf16[27,128,512]{2,1,0:T(8,128)(2,1)} %bitcast.268, bf16[512,256]{1,0:T(8,128)(2,1)} %bitcast.56, bf16[512,256]{1,0:T(8,128)(2,1)S(1)} %maximum_select_fusion.4, pred[]{:T(512)S(6)} %eq.6), kind=kOutput, calls=%fused_computation.34 | convolution fusion | flops 1814298624 | bytes 11141121 | tf_op jit(solution)/shard_map/dot_general | solution.py:100
  147.4 3.4 %collective-permute-start.4 = (bf16[1,1,16,16,512]{4,3,2,1,0:T(8,128)(2,1)S(1)}, bf16[1,1,16,16,512]{4,3,2,1,0:T(8,128)(2,1)S(1)}, u32[]{:S(2)}, u32[]{:S(2)}) collective-permute-start(bf16[1,1,16,16,512]{4,3,2,1,0:T(8,128)(2,1)S(1)} %get-tuple-element.3), channel_id=1, source_target_pairs={{0,2},{1,3},{4,6},{5,7},{8,10},{9,11},{12,14},{13,15},{16,18},{17,... | collective-permute-start | bytes 786440 | tf_op jit(solution)/shard_map/ppermute | solution.py:17
  150.8 1.5 collective-permute-start.5
  152.2 4.2 %collective-permute-done.4 = bf16[1,1,16,16,512]{4,3,2,1,0:T(8,128)(2,1)S(1)} collective-permute-done((bf16[1,1,16,16,512]{4,3,2,1,0:T(8,128)(2,1)S(1)}, bf16[1,1,16,16,512]{4,3,2,1,0:T(8,128)(2,1)S(1)}, u32[]{:S(2)}, u32[]{:S(2)}) %collective-permute-start.4) | collective-permute-done | bytes 262176 | tf_op jit(solution)/shard_map/ppermute | solution.py:17
  156.4 4.1 %collective-permute-done.5 = bf16[1,1,16,16,512]{4,3,2,1,0:T(8,128)(2,1)S(1)} collective-permute-done((bf16[1,1,16,16,512]{4,3,2,1,0:T(8,128)(2,1)S(1)}, bf16[1,1,16,16,512]{4,3,2,1,0:T(8,128)(2,1)S(1)}, u32[]{:S(2)}, u32[]{:S(2)}) %collective-permute-start.5) | collective-permute-done | bytes 262176 | tf_op jit(solution)/shard_map/ppermute | solution.py:18
  160.6 6.7 %convolution_bitcast_fusion = f32[1,4,18,18,27,128]{5,3,4,2,1,0:T(8,128)S(1)} fusion(bf16[27,128,512]{2,1,0:T(8,128)(2,1)S(1)} %copy-done, bf16[1,1,16,16,512]{4,3,2,1,0:T(8,128)(2,1)S(1)} %collective-permute-done.5, bf16[1,2,16,16,512]{4,3,2,1,0:T(8,128)(2,1)S(1)} %maximum_select_fusion, bf16[1,1,16,16,512]{4,3,2,1,0:T(8,128)(2,1)S(1)} %collective-permute-done.4), kind=kOutput, calls=%fused_computation | convolution fusion | flops 4599078912 | bytes 22503424 | tf_op jit(solution)/shard_map/dot_general | solution.py:82
  168.5 38.5 %reduce-scatter.5.cloned.1.call-done = f32[27,128,128]{2,1,0:T(8,128)} async-done(((f32[27,128,512]{2,1,0:T(8,128)}), f32[27,128,128]{2,1,0:T(8,128)}) %reduce-scatter.5.cloned.1.call-update) | async-done | bytes 1769488 | tf_op jit(solution)/shard_map/reduce_scatter | solution.py:104
  207.0 2.9 %broadcast_multiply_fusion = f32[27,128,128]{2,1,0:T(8,128)} fusion(f32[27,128,128]{2,1,0:T(8,128)} %reduce-scatter.5.cloned.1.call-done), kind=kLoop, calls=%fused_computation.27 | loop fusion | flops 442368 | bytes 3538944 | tf_op jit(solution)/shard_map/mul | solution.py:106
  (74 shorter events, 21.2 us)
Async XLA Ops:
  7.2 75.4 %copy-start = (bf16[27,128,512]{2,1,0:T(8,128)(2,1)S(1)}, bf16[27,128,512]{2,1,0:T(8,128)(2,1)}, u32[]{:S(2)}) copy-start(bf16[27,128,512]{2,1,0:T(8,128)(2,1)} %param.5) | copy-start | bytes 10616836
  7.2 107.9 %reduce-scatter.3.cloned.1.call-start = ((), (), s32[]{:S(2)}) async-start(), calls=%async_computation.2 | async-start | bytes 1310720 | tf_op jit(solution)/shard_map/reduce_scatter | solution.py:46
  8.9 8.4 %collective-permute-start = (bf16[1,1,16,16,128]{4,3,2,1,0:T(8,128)(2,1)}, bf16[1,1,16,16,128]{4,3,2,1,0:T(8,128)(2,1)}, u32[]{:S(2)}, u32[]{:S(2)}) collective-permute-start(bf16[1,1,16,16,128]{4,3,2,1,0:T(8,128)(2,1)} %get-tuple-element.33), channel_id=1, source_target_pairs={{0,2},{1,3},{4,6},{5,7},{8,10},{9,11},{12,14},{13,15},{16,18},{17,... | collective-permute-start | bytes 196616 | tf_op jit(solution)/shard_map/ppermute | solution.py:17
  14.4 6.5 %collective-permute-start.1 = (bf16[1,1,16,16,128]{4,3,2,1,0:T(8,128)(2,1)}, bf16[1,1,16,16,128]{4,3,2,1,0:T(8,128)(2,1)}, u32[]{:S(2)}, u32[]{:S(2)}) collective-permute-start(bf16[1,1,16,16,128]{4,3,2,1,0:T(8,128)(2,1)} %get-tuple-element.34), channel_id=1, source_target_pairs={{2,0},{3,1},{6,4},{7,5},{10,8},{11,9},{14,12},{15,13},{18,16},{19,... | collective-permute-start | bytes 196616 | tf_op jit(solution)/shard_map/ppermute | solution.py:18
  17.3 7.0 %copy-start.2 = (bf16[1,2,16,16,128]{4,3,2,1,0:T(8,128)(2,1)S(1)}, bf16[1,2,16,16,128]{4,3,2,1,0:T(8,128)(2,1)}, u32[]{:S(2)}) copy-start(bf16[1,2,16,16,128]{4,3,2,1,0:T(8,128)(2,1)} %param.4) | copy-start | bytes 393220
  69.0 13.1 %copy-start.15 = (bf16[512,128]{0,1:T(8,128)(2,1)S(1)}, bf16[512,128]{0,1:T(8,128)(2,1)}, u32[]{:S(2)}) copy-start(bf16[512,128]{0,1:T(8,128)(2,1)} %copy.21) | copy-start | bytes 393220
  69.0 13.1 %copy-start.14 = (bf16[512,128]{0,1:T(8,128)(2,1)S(1)}, bf16[512,128]{0,1:T(8,128)(2,1)}, u32[]{:S(2)}) copy-start(bf16[512,128]{0,1:T(8,128)(2,1)} %copy.22) | copy-start | bytes 393220
  69.0 13.2 %copy-start.13 = (bf16[512,128]{0,1:T(8,128)(2,1)S(1)}, bf16[512,128]{0,1:T(8,128)(2,1)}, u32[]{:S(2)}) copy-start(bf16[512,128]{0,1:T(8,128)(2,1)} %copy.23) | copy-start | bytes 393220
  69.0 13.2 %copy-start.12 = (bf16[512,128]{0,1:T(8,128)(2,1)S(1)}, bf16[512,128]{0,1:T(8,128)(2,1)}, u32[]{:S(2)}) copy-start(bf16[512,128]{0,1:T(8,128)(2,1)} %copy.24) | copy-start | bytes 393220
  69.1 13.2 %copy-start.11 = (bf16[512,128]{0,1:T(8,128)(2,1)S(1)}, bf16[512,128]{0,1:T(8,128)(2,1)}, u32[]{:S(2)}) copy-start(bf16[512,128]{0,1:T(8,128)(2,1)} %copy.25) | copy-start | bytes 393220
  69.1 13.2 %copy-start.10 = (bf16[512,128]{0,1:T(8,128)(2,1)S(1)}, bf16[512,128]{0,1:T(8,128)(2,1)}, u32[]{:S(2)}) copy-start(bf16[512,128]{0,1:T(8,128)(2,1)} %copy.26) | copy-start | bytes 393220
  69.1 13.2 %copy-start.9 = (bf16[512,128]{0,1:T(8,128)(2,1)S(1)}, bf16[512,128]{0,1:T(8,128)(2,1)}, u32[]{:S(2)}) copy-start(bf16[512,128]{0,1:T(8,128)(2,1)} %copy.27) | copy-start | bytes 393220
  69.1 13.3 %copy-start.8 = (bf16[512,128]{0,1:T(8,128)(2,1)S(1)}, bf16[512,128]{0,1:T(8,128)(2,1)}, u32[]{:S(2)}) copy-start(bf16[512,128]{0,1:T(8,128)(2,1)} %copy.28) | copy-start | bytes 393220
  69.1 13.3 %copy-start.3 = (bf16[512,128]{0,1:T(8,128)(2,1)S(1)}, bf16[512,128]{0,1:T(8,128)(2,1)}, u32[]{:S(2)}) copy-start(bf16[512,128]{0,1:T(8,128)(2,1)} %copy.29) | copy-start | bytes 393220
  69.1 13.3 %copy-start.7 = (bf16[512,128]{0,1:T(8,128)(2,1)S(1)}, bf16[512,128]{0,1:T(8,128)(2,1)}, u32[]{:S(2)}) copy-start(bf16[512,128]{0,1:T(8,128)(2,1)} %copy.30) | copy-start | bytes 393220
  69.1 13.3 %copy-start.6 = (bf16[512,128]{0,1:T(8,128)(2,1)S(1)}, bf16[512,128]{0,1:T(8,128)(2,1)}, u32[]{:S(2)}) copy-start(bf16[512,128]{0,1:T(8,128)(2,1)} %copy.31) | copy-start | bytes 393220
  69.1 13.3 %copy-start.5 = (bf16[512,128]{0,1:T(8,128)(2,1)S(1)}, bf16[512,128]{0,1:T(8,128)(2,1)}, u32[]{:S(2)}) copy-start(bf16[512,128]{0,1:T(8,128)(2,1)} %copy.32) | copy-start | bytes 393220
  69.1 13.4 %copy-start.4 = (bf16[512,128]{0,1:T(8,128)(2,1)S(1)}, bf16[512,128]{0,1:T(8,128)(2,1)}, u32[]{:S(2)}) copy-start(bf16[512,128]{0,1:T(8,128)(2,1)} %copy.33) | copy-start | bytes 393220
  82.5 1.9 copy-start.1
  84.4 30.7 %copy-start.16 = (f32[128]{0:T(128)S(1)}, f32[128]{0:T(128)}, u32[]{:S(2)}) copy-start(f32[128]{0:T(128)} %param.6) | copy-start | bytes 1540
  87.5 119.5 %reduce-scatter.5.cloned.1.call-start = ((), (), s32[]{:S(2)}) async-start(), calls=%async_computation.3 | async-start | bytes 8847360 | tf_op jit(solution)/shard_map/reduce_scatter | solution.py:104
  116.9 5.4 %collective-permute-start.2 = (bf16[1,2,16,16,128]{4,3,2,1,0:T(8,128)(2,1)}, bf16[1,2,16,16,128]{4,3,2,1,0:T(8,128)(2,1)}, u32[]{:S(2)}, u32[]{:S(2)}) collective-permute-start(bf16[1,2,16,16,128]{4,3,2,1,0:T(8,128)(2,1)} %bitcast.33), channel_id=1, source_target_pairs={{0,4},{4,0},{8,12},{12,8},{1,5},{5,1},{9,13},{13,9},{2,6},{6,2},{1... | collective-permute-start | bytes 393224 | tf_op jit(solution)/shard_map/ppermute | solution.py:72
  124.2 13.8 %collective-permute-start.3 = (bf16[1,2,16,16,256]{4,3,2,1,0:T(8,128)(2,1)}, bf16[1,2,16,16,256]{4,3,2,1,0:T(8,128)(2,1)}, u32[]{:S(2)}, u32[]{:S(2)}) collective-permute-start(bf16[1,2,16,16,256]{4,3,2,1,0:T(8,128)(2,1)} %maximum_select_fusion.3), channel_id=1, source_target_pairs={{0,8},{4,12},{8,0},{12,4},{1,9},{5,13},{9,1},{13,5},{2,10},{6,14},... | collective-permute-start | bytes 786440 | tf_op jit(solution)/shard_map/ppermute | solution.py:72
  147.4 9.1 %collective-permute-start.4 = (bf16[1,1,16,16,512]{4,3,2,1,0:T(8,128)(2,1)S(1)}, bf16[1,1,16,16,512]{4,3,2,1,0:T(8,128)(2,1)S(1)}, u32[]{:S(2)}, u32[]{:S(2)}) collective-permute-start(bf16[1,1,16,16,512]{4,3,2,1,0:T(8,128)(2,1)S(1)} %get-tuple-element.3), channel_id=1, source_target_pairs={{0,2},{1,3},{4,6},{5,7},{8,10},{9,11},{12,14},{13,15},{16,18},{17,... | collective-permute-start | bytes 786440 | tf_op jit(solution)/shard_map/ppermute | solution.py:17
  150.8 9.8 %collective-permute-start.5 = (bf16[1,1,16,16,512]{4,3,2,1,0:T(8,128)(2,1)S(1)}, bf16[1,1,16,16,512]{4,3,2,1,0:T(8,128)(2,1)S(1)}, u32[]{:S(2)}, u32[]{:S(2)}) collective-permute-start(bf16[1,1,16,16,512]{4,3,2,1,0:T(8,128)(2,1)S(1)} %get-tuple-element.4), channel_id=1, source_target_pairs={{2,0},{3,1},{6,4},{7,5},{10,8},{11,9},{14,12},{15,13},{18,16},{19,... | collective-permute-start | bytes 786440 | tf_op jit(solution)/shard_map/ppermute | solution.py:18
Sparse Core Ops, SparseCore 0:
  87.6 27.4 reduce-scatter.2
  145.1 61.8 reduce-scatter.4
